TPU v7x, 32 devices: a whole 2x2x4 slice. The times are simulated.
32 devices in a mesh: leaf: 8 (over z, y), rhs: 4 (over x, core).
Axes of the slice: x: 2, y: 2, z: 4, core: 2. Of those that a mesh axis runs over, the one named last changes fastest.
Arguments:
- rhs_block: float32 [4096, 1024], P('leaf', 'rhs'), may hold values from -6 to 6
- leaf_order: int32 [8, 512], P('leaf'), may hold values from 0 to 511, as said below
- leaf_inverse: float32 [4096, 512], P('leaf'), may hold values from -0.04 to 3, as said below
- leaf_basis: float32 [4096, 128], P('leaf'), may hold values from -0.09678524 to 0.09678524
- transfer: bfloat16 [8, 2, 128, 128], P('leaf'), may hold values from -0.05 to 1.25, as said below
- precision: bfloat16 [8, 3, 128, 128], P('leaf'), may hold values from -0.09 to 8, as said below
Outputs:
- solution: float32 [4096, 1024], P('leaf', 'rhs')
Inputs may be any that keep to these rules, and one draw needn't show every extreme that they name: `leaf_order`: each row is a permutation of 0 to 511. `leaf_inverse`: each leaf's block of 512 x 512 entries is symmetric positive definite. transfer[b, k] is the same for all leaves b of one aligned group of 2 ** (k + 1) leaves. Every block is symmetric positive definite; precision[b, k] is the same for all leaves b of one aligned group of 2 ** (k + 1) leaves.
All inputs are finite; a program needn't handle non-finite values.
Results may differ from a plain program's by a relative error of at most 0.0003.
Values sent between devices are 32-bit elements; how exact they have to be, the bound alone decides.
No kernel may reach another device: no remote copies, remote signals or barrier semaphores. Data moves between devices by JAX's collectives and lax.ppermute only.
A program may use at most 64 MiB of HBM per device.

v0:
```python
import functools

import jax
import jax.numpy as jnp
from jax import lax
from jax.experimental import pallas as pl
from jax.experimental.pallas import tpu as pltpu
from jax.sharding import PartitionSpec as P

F32 = jnp.float32
BF16 = jnp.bfloat16
HIGH = lax.Precision.HIGH
SUB = 8
GIGA = 10 ** 9
VMEM = pl.BlockSpec(memory_space=pltpu.VMEM)
FAR = pl.BlockSpec(memory_space=pltpu.HBM)
PARAMS = pltpu.CompilerParams(vmem_limit_bytes=32 * 1024 * 1024)


def mm(a, b, precision=HIGH, dims=((1,), (0,))):
    return lax.dot_general(a, b, (dims, ((), ())), precision=precision, preferred_element_type=F32)


def split(x):
    top = x.astype(BF16)
    return top, (x - top.astype(F32)).astype(BF16)


def mm_parts(a, b):
    columns = b[0].shape[1]
    both = jnp.dot(a[0], jnp.concatenate(b, axis=1), preferred_element_type=F32)
    return both[:, :columns] + (both[:, columns:] + jnp.dot(a[1], b[0], preferred_element_type=F32))


def pick(mask, x):
    top, low = split(x)
    one = lambda part: lax.dot_general(mask, part, (((1,), (0,)), ((), ())), preferred_element_type=F32)
    return one(top) + one(low)


def reciprocal(x):
    return pltpu.reciprocal(x, approx=True)

def parts(x):
    top = x.astype(BF16).astype(F32)
    rest = x - top
    mid = rest.astype(BF16).astype(F32)
    return top, mid, rest - mid

def spread(x, k):
    return jnp.broadcast_to(x[:, k:k + 1], x.shape)


def four(x, y, cols, at, k, lane, row, hold):
    size = x.shape[1]
    across = size // SUB * SUB
    inside = (lane >= k) & (lane < k + 4)
    own = (row >= at) & (row < at + 4)
    ahead = [(k + 4 + j) % across for j in range(4)]
    coming = [spread(x, a) for a in ahead]
    down = [spread(y, k + j) for j in range(4)]
    for j, tile in enumerate([*cols, *coming, x]):
        hold[j * SUB:(j + 1) * SUB] = tile
    line = lambda j, i: hold[pl.ds(j * SUB + at + i, SUB, stride=0)]
    a0, a1, a2 = line(0, 0), line(1, 0), line(1, 1)
    b00, b01, b10, b11 = line(0, 2), line(1, 2), line(0, 3), line(1, 3)
    c0, c1, c2 = line(2, 2), line(3, 2), line(3, 3)
    det = a0 * a2 - a1 * a1
    g00, g01 = b00 * a2 - b01 * a1, b01 * a0 - b00 * a1
    g10, g11 = b10 * a2 - b11 * a1, b11 * a0 - b10 * a1
    s0 = det * c0 - (g00 * b00 + g01 * b01)
    s1 = det * c1 - (g00 * b10 + g01 * b11)
    s2 = det * c2 - (g10 * b10 + g11 * b11)
    rs = reciprocal(s0 * s2 - s1 * s1)
    ra = reciprocal(det)

    def known(e):
        t2 = det * e[2] - (g00 * e[0] + g01 * e[1])
        t3 = det * e[3] - (g10 * e[0] + g11 * e[1])
        return a2 * e[0] - a1 * e[1], a0 * e[1] - a1 * e[0], s2 * t2 - s1 * t3, s0 * t3 - s1 * t2

    def second(c):
        return c[0], c[1], c[2] - (c[0] * g00 + c[1] * g01) * ra, c[3] - (c[0] * g10 + c[1] * g11) * ra

    def less(base, c, v):
        return (base - (c[0] * v[0] + c[1] * v[1]) * ra) - (c[2] * v[2] + c[3] * v[3]) * rs

    cols = second([jnp.where(own, jnp.where(row == at + j, -1.0, 0.0), cols[j]) for j in range(4)])
    down = second(down)
    there = [known([line(4 + j, i) for i in range(4)]) for j in range(4)]
    if at + 4 < SUB:
        after = [less(jnp.where(own, 0.0, coming[j]), cols, there[j]) for j in range(4)]
    else:
        after = [less(spread(y, ahead[j]), down, there[j]) for j in range(4)]
    here = known([jnp.where(inside, jnp.where(lane == k + j, 1.0, 0.0), line(8, j)) for j in range(4)])
    x = less(jnp.where(inside | own, 0.0, x), cols, here)
    y = less(jnp.where(inside, 0.0, y), down, here)
    return x, y, after


def invert(m, xt, w6, hold):
    size = m.shape[0]
    lane = lax.broadcasted_iota(jnp.int32, (SUB, size), 1)
    row = lax.broadcasted_iota(jnp.int32, (SUB, size), 0)
    wide = lax.broadcasted_iota(jnp.int32, (size, size), 1)
    eye = jnp.where(wide == lax.broadcasted_iota(jnp.int32, (size, size), 0), 1.0, 0.0).astype(BF16)
    count = size // SUB

    def trail(t):
        k = t * SUB
        u = jnp.dot(xt[...], w6[...], preferred_element_type=F32)
        new = jnp.where((wide >= k) & (wide < k + SUB), 0.0, m[...]) - u
        m[...] = new
        return new

    def step(t, carry):
        x, *cols = carry
        k = t * SUB
        after = (t + 1) % count * SUB
        y = trail(t - 1)[after:after + SUB] if t else m[SUB:2 * SUB]
        z = jnp.where(lane < k, -1.0, 1.0) * x
        z = jnp.where((lane >= k) & (lane < k + SUB), jnp.where(lane - k == row, -1.0, 0.0), z)
        h, n, l = parts(z)
        z = jnp.concatenate([h, h, n, n, h, l], axis=0).astype(BF16)
        xt[...] = lax.dot_general(eye, z, (((1,), (1,)), ((), ())), preferred_element_type=F32).astype(BF16)
        for g in range(0, SUB, 4):
            x, y, cols = four(x, y, cols, g, k + g, lane, row, hold.at[g // 4])
        h, n, l = parts(x)
        w6[...] = jnp.concatenate([h, n, h, n, l, h], axis=0).astype(BF16)
        m[pl.ds(k, SUB)] = jnp.zeros((SUB, size), F32)
        return y, *cols

    x = m[0:SUB]
    carry = (x, *(spread(x, j) for j in range(4)))
    for t in range(count):
        carry = step(t, carry)
    trail(count - 1)


def invert_scratch(size):
    return [
        pltpu.VMEM((size, size), F32), pltpu.VMEM((size, 6 * SUB), BF16), pltpu.VMEM((6 * SUB, size), BF16),
        pltpu.VMEM((SUB // 4, 10 * SUB, size), F32),
    ]


def scaled_inverse(matrix, *work):
    size = matrix.shape[0]
    rows = lax.broadcasted_iota(jnp.int32, (size, size), 0)
    cols = lax.broadcasted_iota(jnp.int32, (size, size), 1)
    diagonal = jnp.where(rows == cols, matrix, 0.0)
    down = lax.rsqrt(jnp.sum(diagonal, axis=1, keepdims=True))
    across = lax.rsqrt(jnp.sum(diagonal, axis=0, keepdims=True))
    work[0][...] = matrix * down * across
    invert(*work)
    return work[0][...] * down * across


def fold(gram):
    size = gram.shape[0]
    half = size // 2
    rows = lax.broadcasted_iota(jnp.int32, (half, size), 0)
    cols = lax.broadcasted_iota(jnp.int32, (half, size), 1)
    low = gram[half:]
    body = jnp.where(cols < rows, pltpu.roll(low, half, 1), gram[:half])
    diagonal = jnp.sum(jnp.where(cols == rows + half, low, 0.0), axis=0, keepdims=True)
    return jnp.concatenate([body, jnp.where(rows[:SUB] == 0, diagonal, 0.0)], axis=0)


def unfold(folded):
    size = folded.shape[1]
    half = size // 2
    rows = lax.broadcasted_iota(jnp.int32, (size, size), 0)
    cols = lax.broadcasted_iota(jnp.int32, (size, size), 1)
    body = folded[:half]
    below = cols[:half] < rows[:half]
    low = pltpu.roll(jnp.where(below, body, 0.0), half, 1)
    low = jnp.where(cols[:half] == rows[:half] + half, folded[half:half + 1], low)
    upper = jnp.concatenate([jnp.where(below, 0.0, body), low], axis=0)
    return upper + jnp.where(rows == cols, 0.0, upper.T)


def basis_kernel(pieces, inverse_far, basis_far, order_far, top, low, basis_t, order, carried, gram, inverse, basis, sems):
    rows = inverse.shape[0] // pieces
    copies = [pltpu.make_async_copy(basis_far, basis, sems.at[pieces])]
    for i in range(pieces):
        part = pl.ds(i * rows, rows)
        copies.append(pltpu.make_async_copy(inverse_far.at[part], inverse.at[part], sems.at[i]))
    copies.append(pltpu.make_async_copy(order_far, order, sems.at[pieces + 1]))
    for copy in copies:
        copy.start()
    copies[0].wait()
    basis_parts = split(basis[...])
    across = basis[...].T
    basis_t[...] = across
    across = split(across)
    for i in range(pieces):
        part = slice(i * rows, (i + 1) * rows)
        copies[i + 1].wait()
        block = split(inverse[part])
        top[part], low[part] = block
        carried[part] = mm_parts(block, basis_parts)
    gram[...] = fold(mm_parts(across, split(carried[...])))
    copies[-1].wait()


def leaf_kernel(order, rhs, top, low, basis_t, solved, projected):
    points = rhs.shape[0]
    wide = 128
    numbers = order[...].astype(F32)
    lanes = lax.broadcasted_iota(jnp.int32, (wide, points), 1).astype(F32)
    gather = []
    for i in range(0, points, wide):
        column = jnp.broadcast_to(numbers[:, i:i + wide], (wide, wide)).T
        column = jnp.concatenate([column] * (points // wide), axis=1)
        gather.append(jnp.where(column == lanes, 1.0, 0.0).astype(BF16))
    ordered = pick(jnp.concatenate(gather, axis=0), rhs[...])
    z = mm_parts((top[...], low[...]), split(ordered))
    solved[...] = z
    projected[...] = mm(basis_t[...], z)


def node_kernel(level, gram, other, precision, *rest):
    coupling = precision[0, level].astype(F32)
    whole = unfold(gram[...] + other[...])
    if len(rest) == 5:
        rest[0][...] = scaled_inverse(coupling + whole, *rest[1:])
        return
    transfer, inverse, mover, gram_out, *work = rest
    mixer = transfer[0, level]
    left = mm(mixer, precision[0, level], None, ((0,), (0,)))
    right = sum(mm(part.astype(BF16), mixer, None) for part in parts(whole))
    m = scaled_inverse(coupling + whole, *work)
    n = mm(left, m)
    inverse[...] = m
    mover[...] = n
    gram_out[...] = fold(mm(n, right))


def lift_kernel(first, last, *refs):
    refs = list(refs)
    projected, other, inverse, mover = (refs.pop(0)[...] for _ in range(4))
    s = projected + other
    alpha = mm(inverse, s)
    outs = refs[-5:] if first and not last else refs[-3:]
    outs[0][...] = mm(mover, s)
    if first:
        order, solved, carried = (refs.pop(0)[...] for _ in range(3))
        points = solved.shape[0]
        rows = lax.broadcasted_iota(jnp.int32, (points, points), 0)
        scatter = jnp.where(order == rows, 1.0, 0.0).astype(BF16)
        solved, carried = pick(scatter, solved), pick(scatter, carried)
        total, mixing = alpha, mover.T
    else:
        total, mixing, solved, carried = (refs.pop(0)[...] for _ in range(4))
        total = total + mm(mixing, alpha)
        mixing = mm(mixing, mover, HIGH, ((1,), (1,)))
    if last:
        total = solved - mm(carried, total)
        mixing = mm(carried, mixing)
    outs[1][...] = total
    outs[2][...] = mixing
    if first and not last:
        outs[3][...] = solved
        outs[4][...] = carried


def root_kernel(pieces, projected, other, inverse, solved, carried, out_far, out, sems):
    alpha = mm(inverse[...], projected[...] + other[...])
    rows = out.shape[0] // pieces
    copies = []
    for i in range(pieces):
        part = pl.ds(i * rows, rows)
        out[part] = solved[part] - mm(carried[part], alpha)
        copies.append(pltpu.make_async_copy(out.at[part], out_far.at[part], sems.at[i]))
        copies[-1].start()
    for copy in copies:
        copy.wait()


def call(kernel, outs, *args, scratch=(), work=0, place=VMEM, result=VMEM):
    if place is FAR:
        args = [pltpu.with_memory_space_constraint(arg, pltpu.HBM) for arg in args]
    return pl.pallas_call(
        kernel,
        out_shape=[jax.ShapeDtypeStruct(getattr(out, "shape", out), getattr(out, "dtype", F32)) for out in outs],
        in_specs=[place] * len(args),
        out_specs=[result] * len(outs),
        scratch_shapes=scratch,
        cost_estimate=pl.CostEstimate(flops=work, bytes_accessed=0, transcendentals=0),
        compiler_params=PARAMS,
    )(*args)


def from_partner(block, axis, apart):
    count = lax.axis_size(axis)
    return lax.ppermute(block, axis, [(i, i ^ 1 << apart) for i in range(count)])


def body(rhs, order, inverse, basis, transfer, precision):
    points, columns = rhs.shape
    rank = basis.shape[1]
    square, tall, block = (rank, rank), (points, rank), (rank, columns)
    folded = (rank // 2 + SUB, rank)
    levels = lax.axis_size("leaf").bit_length() - 1
    pieces = 2
    half = jax.ShapeDtypeStruct(inverse.shape, BF16)
    top, low, basis_t, order, carried, gram = call(
        functools.partial(basis_kernel, pieces), [half, half, (rank, points), order, tall, folded],
        inverse, basis, order, place=FAR, work=GIGA,
        scratch=[pltpu.VMEM(inverse.shape, F32), pltpu.VMEM(tall, F32), pltpu.SemaphoreType.DMA((pieces + 2,))]
    )
    other_gram = from_partner(gram, "leaf", 0)
    solved, projected = call(leaf_kernel, [rhs, block], order, rhs, top, low, basis_t, work=2 * GIGA)
    if levels == 1:
        raise NotImplementedError("one level")
    state = [order, solved, carried]
    for k in range(levels - 1):
        other = from_partner(projected, "leaf", k)
        m, n, gram = call(
            functools.partial(node_kernel, k), [square, square, folded], gram, other_gram, precision, transfer,
            scratch=invert_scratch(rank), work=6 * GIGA
        )
        other_gram = from_partner(gram, "leaf", k + 1)
        first, last = k == 0, k == levels - 2
        outs = [rhs, tall] if last else [block, square, rhs, tall] if first else [block, square]
        projected, *new = call(
            functools.partial(lift_kernel, first, last), [block] + outs, projected, other, m, n, *state, work=GIGA
        )
        state = new + state[len(new):]
    solved, carried = state[:2]
    k = levels - 1
    other = from_partner(projected, "leaf", k)
    (m,) = call(functools.partial(node_kernel, k), [square], gram, other_gram, precision, scratch=invert_scratch(rank), work=6 * GIGA)
    (out,) = call(
        functools.partial(root_kernel, 2 * pieces), [rhs], projected, other, m, solved, carried, work=GIGA, result=FAR,
        scratch=[pltpu.VMEM(rhs.shape, F32), pltpu.SemaphoreType.DMA((2 * pieces,))]
    )
    return out


def solution(mesh):
    placed = (
        P("leaf", "rhs"),
        P("leaf", None),
        P("leaf", None),
        P("leaf", None),
        P("leaf", None, None, None),
        P("leaf", None, None, None),
    )
    return jax.shard_map(
        body, mesh=mesh, in_specs=placed, out_specs=P("leaf", "rhs"), check_vma=False
    )
```

profile of v0, /device:TPU:0, one launch (start us, length us, event | category | flops | bytes accessed | tf_op | source)
XLA Modules:
  0.0 31.0 jit_solution(9304349639717106154)
XLA Ops:
  0.0 0.0 copy-start
  0.0 2.1 %shard_map.64 = (bf16[512,512]{1,0:T(8,128)(2,1)S(1)}, bf16[512,512]{1,0:T(8,128)(2,1)S(1)}, f32[128,512]{1,0:T(8,128)S(1)}, s32[1,512]{1,0:T(1,128)S(1)}, f32[5...) custom-call(f32[512,512]{1,0:T(8,128)} %inverse_far.1, f32[512,128]{1,0:T(8,128)} %basis_far.1, s32[1,512]{1,0:T(1,128)} %order_far.1), custom_call_target="tpu_custom_call" | custom-call | flops 1000000000 | tf_op jit(solution)/shard_map/pallas_call | solution.py:284
  2.1 3.0 %collective-permute-start.1 = (f32[72,128]{1,0:T(8,128)S(1)}, f32[72,128]{1,0:T(8,128)S(1)}, u32[]{:S(2)}, u32[]{:S(2)}) collective-permute-start(f32[72,128]{1,0:T(8,128)S(1)} %get-tuple-element.32.gram), channel_id=1, source_target_pairs={{0,4},{4,0},{8,12},{12,8},{16,20},{20,16},{24,28},{28,24},{1,5},{5... | collective-permute-start | bytes 110600 | tf_op jit(solution)/shard_map/ppermute | solution.py:297
  5.1 0.0 copy-done
  5.1 1.8 %shard_map.65 = (f32[512,256]{1,0:T(8,128)S(1)}, f32[128,256]{1,0:T(8,128)S(1)}) custom-call(s32[1,512]{1,0:T(1,128)S(1)} %get-tuple-element.27.order.refs_4_, f32[512,256]{1,0:T(8,128)S(1)} %copy-done, bf16[512,512]{1,0:T(8,128)(2,1)S(1)} %get-tuple-element.28.top, bf16[512,512]{1,0:T(8,128)(2,1)S(1)} %get-tuple-element.29.low, ...), custom_call_target="tpu_custom_call" | custom-call | flops 2000000000 | tf_op jit(solution)/shard_map/pallas_call | solution.py:284
  6.9 0.1 collective-permute-start
  7.0 0.0 collective-permute-done.1.other
  7.0 0.0 copy-done.1
  7.0 0.0 copy-done.2
  7.0 4.3 %shard_map.66 = (f32[128,128]{1,0:T(8,128)S(1)}, f32[128,128]{1,0:T(8,128)S(1)}, f32[72,128]{1,0:T(8,128)S(1)}) custom-call(f32[72,128]{1,0:T(8,128)S(1)} %get-tuple-element.32.gram, f32[72,128]{1,0:T(8,128)S(1)} %collective-permute-done.1.other, bf16[1,3,128,128]{3,2,1,0:T(8,128)(2,1)S(1)} %copy-done.1, bf16[1,2,128,128]{3,2,1,0:T(8,128)(2,1)S(1)} %copy-done.2), custom_call_target="tpu_custom_call" | custom-call | flops 6000000000 | tf_op jit(solution)/shard_map/pallas_call | solution.py:284
  11.3 2.1 %collective-permute-start.3 = (f32[72,128]{1,0:T(8,128)S(1)}, f32[72,128]{1,0:T(8,128)S(1)}, u32[]{:S(2)}, u32[]{:S(2)}) collective-permute-start(f32[72,128]{1,0:T(8,128)S(1)} %get-tuple-element.38.gram), channel_id=1, source_target_pairs={{0,8},{4,12},{8,0},{12,4},{16,24},{20,28},{24,16},{28,20},{1,9},{5... | collective-permute-start | bytes 110600 | tf_op jit(solution)/shard_map/ppermute | solution.py:297
  13.5 0.0 collective-permute-done.refs_1_
  13.5 0.8 %shard_map.67 = (f32[128,256]{1,0:T(8,128)S(1)}, f32[128,256]{1,0:T(8,128)S(1)}, f32[128,128]{1,0:T(8,128)S(1)}, f32[512,256]{1,0:T(8,128)S(1)}, f32[512,128]{1,0:T(8,128)S(1)}) custom-call(f32[128,256]{1,0:T(8,128)S(1)} %get-tuple-element.31.refs_0_, f32[128,256]{1,0:T(8,128)S(1)} %collective-permute-done.refs_1_, ...), custom_call_target="tpu_custom_call" | custom-call | flops 1000000000 | tf_op jit(solution)/shard_map/pallas_call | solution.py:284
  14.3 0.1 collective-permute-start.2
  14.4 1.0 %collective-permute-done.3.other = f32[72,128]{1,0:T(8,128)S(1)} collective-permute-done((f32[72,128]{1,0:T(8,128)S(1)}, f32[72,128]{1,0:T(8,128)S(1)}, u32[]{:S(2)}, u32[]{:S(2)}) %collective-permute-start.3) | collective-permute-done | bytes 36896 | tf_op jit(solution)/shard_map/ppermute | solution.py:297
  15.4 4.3 %shard_map.68 = (f32[128,128]{1,0:T(8,128)S(1)}, f32[128,128]{1,0:T(8,128)S(1)}, f32[72,128]{1,0:T(8,128)S(1)}) custom-call(f32[72,128]{1,0:T(8,128)S(1)} %get-tuple-element.38.gram, f32[72,128]{1,0:T(8,128)S(1)} %collective-permute-done.3.other, bf16[1,3,128,128]{3,2,1,0:T(8,128)(2,1)S(1)} %copy-done.1, bf16[1,2,128,128]{3,2,1,0:T(8,128)(2,1)S(1)} %copy-done.2), custom_call_target="tpu_custom_call" | custom-call | flops 6000000000 | tf_op jit(solution)/shard_map/pallas_call | solution.py:284
  19.7 3.1 %collective-permute-start.5 = (f32[72,128]{1,0:T(8,128)S(1)}, f32[72,128]{1,0:T(8,128)S(1)}, u32[]{:S(2)}, u32[]{:S(2)}) collective-permute-start(f32[72,128]{1,0:T(8,128)S(1)} %get-tuple-element.46.gram), channel_id=1, source_target_pairs={{0,16},{4,20},{8,24},{12,28},{16,0},{20,4},{24,8},{28,12},{1,17},{... | collective-permute-start | bytes 110600 | tf_op jit(solution)/shard_map/ppermute | solution.py:297
  22.8 0.0 collective-permute-done.2.refs_1_
  22.8 0.9 %shard_map.69 = (f32[128,256]{1,0:T(8,128)S(1)}, f32[512,256]{1,0:T(8,128)S(1)}, f32[512,128]{1,0:T(8,128)S(1)}) custom-call(f32[128,256]{1,0:T(8,128)S(1)} %get-tuple-element.37.refs_0_, f32[128,256]{1,0:T(8,128)S(1)} %collective-permute-done.2.refs_1_, f32[128,128]{1,0:T(8,128)S(1)} %get-tuple-element.39.refs_2_, ...), custom_call_target="tpu_custom_call" | custom-call | flops 1000000000 | tf_op jit(solution)/shard_map/pallas_call | solution.py:284
  23.7 0.1 collective-permute-start.4
  23.8 0.9 %collective-permute-done.5.other = f32[72,128]{1,0:T(8,128)S(1)} collective-permute-done((f32[72,128]{1,0:T(8,128)S(1)}, f32[72,128]{1,0:T(8,128)S(1)}, u32[]{:S(2)}, u32[]{:S(2)}) %collective-permute-start.5) | collective-permute-done | bytes 36896 | tf_op jit(solution)/shard_map/ppermute | solution.py:297
  24.7 3.8 %shard_map.70.inverse = f32[128,128]{1,0:T(8,128)S(1)} custom-call(f32[72,128]{1,0:T(8,128)S(1)} %get-tuple-element.46.gram, f32[72,128]{1,0:T(8,128)S(1)} %collective-permute-done.5.other, bf16[1,3,128,128]{3,2,1,0:T(8,128)(2,1)S(1)} %copy-done.1), custom_call_target="tpu_custom_call" | custom-call | flops 6000000000 | tf_op jit(solution)/shard_map/pallas_call | solution.py:284
  28.5 1.1 %collective-permute-done.4.other = f32[128,256]{1,0:T(8,128)S(1)} collective-permute-done((f32[128,256]{1,0:T(8,128)S(1)}, f32[128,256]{1,0:T(8,128)S(1)}, u32[]{:S(2)}, u32[]{:S(2)}) %collective-permute-start.4) | collective-permute-done | bytes 131104 | tf_op jit(solution)/shard_map/ppermute | solution.py:297
  29.7 1.3 %shard_map.71 = f32[512,256]{1,0:T(8,128)} custom-call(f32[128,256]{1,0:T(8,128)S(1)} %get-tuple-element.45.projected, f32[128,256]{1,0:T(8,128)S(1)} %collective-permute-done.4.other, f32[128,128]{1,0:T(8,128)S(1)} %shard_map.70.inverse, f32[512,256]{1,0:T(8,128)S(1)} %get-tuple-element.47.solved, f32[512,128]{1,0:T(8,128)S(1)} %get-tuple-element.48.carried), custom_call_target="tpu_custom_call" | custom-call | flops 1000000000 | tf_op jit(solution)/shard_map/pallas_call | solution.py:284
  (2 shorter events, 0.0 us)
Async XLA Ops:
  0.0 5.1 %copy-start = (f32[512,256]{1,0:T(8,128)S(1)}, f32[512,256]{1,0:T(8,128)}, u32[]{:S(2)}) copy-start(f32[512,256]{1,0:T(8,128)} %rhs.1) | copy-start | bytes 1572868
  2.1 5.0 %collective-permute-start.1 = (f32[72,128]{1,0:T(8,128)S(1)}, f32[72,128]{1,0:T(8,128)S(1)}, u32[]{:S(2)}, u32[]{:S(2)}) collective-permute-start(f32[72,128]{1,0:T(8,128)S(1)} %get-tuple-element.32.gram), channel_id=1, source_target_pairs={{0,4},{4,0},{8,12},{12,8},{16,20},{20,16},{24,28},{28,24},{1,5},{5... | collective-permute-start | bytes 110600 | tf_op jit(solution)/shard_map/ppermute | solution.py:297
  5.1 1.9 %copy-start.1 = (bf16[1,3,128,128]{3,2,1,0:T(8,128)(2,1)S(1)}, bf16[1,3,128,128]{3,2,1,0:T(8,128)(2,1)}, u32[]{:S(2)}) copy-start(bf16[1,3,128,128]{3,2,1,0:T(8,128)(2,1)} %precision.5) | copy-start | bytes 294916
  5.1 1.9 %copy-start.2 = (bf16[1,2,128,128]{3,2,1,0:T(8,128)(2,1)S(1)}, bf16[1,2,128,128]{3,2,1,0:T(8,128)(2,1)}, u32[]{:S(2)}) copy-start(bf16[1,2,128,128]{3,2,1,0:T(8,128)(2,1)} %rest_0_.3) | copy-start | bytes 196612
  6.9 6.5 %collective-permute-start = (f32[128,256]{1,0:T(8,128)S(1)}, f32[128,256]{1,0:T(8,128)S(1)}, u32[]{:S(2)}, u32[]{:S(2)}) collective-permute-start(f32[128,256]{1,0:T(8,128)S(1)} %get-tuple-element.31.refs_0_), channel_id=1, source_target_pairs={{0,4},{4,0},{8,12},{12,8},{16,20},{20,16},{24,28},{28,24},{1,5},{5... | collective-permute-start | bytes 393224 | tf_op jit(solution)/shard_map/ppermute | solution.py:297
  11.3 4.1 %collective-permute-start.3 = (f32[72,128]{1,0:T(8,128)S(1)}, f32[72,128]{1,0:T(8,128)S(1)}, u32[]{:S(2)}, u32[]{:S(2)}) collective-permute-start(f32[72,128]{1,0:T(8,128)S(1)} %get-tuple-element.38.gram), channel_id=1, source_target_pairs={{0,8},{4,12},{8,0},{12,4},{16,24},{20,28},{24,16},{28,20},{1,9},{5... | collective-permute-start | bytes 110600 | tf_op jit(solution)/shard_map/ppermute | solution.py:297
  14.3 8.5 %collective-permute-start.2 = (f32[128,256]{1,0:T(8,128)S(1)}, f32[128,256]{1,0:T(8,128)S(1)}, u32[]{:S(2)}, u32[]{:S(2)}) collective-permute-start(f32[128,256]{1,0:T(8,128)S(1)} %get-tuple-element.37.refs_0_), channel_id=1, source_target_pairs={{0,8},{4,12},{8,0},{12,4},{16,24},{20,28},{24,16},{28,20},{1,9},{5... | collective-permute-start | bytes 393224 | tf_op jit(solution)/shard_map/ppermute | solution.py:297
  19.7 5.0 %collective-permute-start.5 = (f32[72,128]{1,0:T(8,128)S(1)}, f32[72,128]{1,0:T(8,128)S(1)}, u32[]{:S(2)}, u32[]{:S(2)}) collective-permute-start(f32[72,128]{1,0:T(8,128)S(1)} %get-tuple-element.46.gram), channel_id=1, source_target_pairs={{0,16},{4,20},{8,24},{12,28},{16,0},{20,4},{24,8},{28,12},{1,17},{... | collective-permute-start | bytes 110600 | tf_op jit(solution)/shard_map/ppermute | solution.py:297
  23.7 6.0 %collective-permute-start.4 = (f32[128,256]{1,0:T(8,128)S(1)}, f32[128,256]{1,0:T(8,128)S(1)}, u32[]{:S(2)}, u32[]{:S(2)}) collective-permute-start(f32[128,256]{1,0:T(8,128)S(1)} %get-tuple-element.45.projected), channel_id=1, source_target_pairs={{0,16},{4,20},{8,24},{12,28},{16,0},{20,4},{24,8},{28,12},{1,17},{... | collective-permute-start | bytes 393224 | tf_op jit(solution)/shard_map/ppermute | solution.py:297
where the time goes:
time: 31.1 us; the launch traced here: 31 us
  Pallas kernels  19.2 us (62%)
  starting transfers between devices  8.6 us (28%)
  waiting for transfers between devices  3.08 us (10%)
    pallas_call x8, Pallas kernels, call(): pl.pallas_call(kernel, out_shape=[jax.ShapeDtypeStruct(getattr(out, 'shap...  19.2 us
    ppermute x6, starting transfers between devices, from_partner(): lax.ppermute(block, axis, [(i, i ^ 1 << apart) for i in range(count)])  8.6 us
    ppermute x6, waiting for transfers between devices, from_partner(): lax.ppermute(block, axis, [(i, i ^ 1 << apart) for i in range(count)])  3.08 us
  transfers between devices with their start and end apart: 6, of which 3 were waited for; matrix products, arithmetic and copies ran while one was open for 0% of the time, Pallas kernels for 51%

commit v1 on v0

--- a/solution.py
+++ b/solution.py
@@ -51,15 +51,13 @@
     return jnp.broadcast_to(x[:, k:k + 1], x.shape)
 
 
-def four(x, y, cols, at, k, lane, row, hold):
+def four(x, y, at, k, lane, row, hold):
     size = x.shape[1]
-    across = size // SUB * SUB
     inside = (lane >= k) & (lane < k + 4)
     own = (row >= at) & (row < at + 4)
-    ahead = [(k + 4 + j) % across for j in range(4)]
-    coming = [spread(x, a) for a in ahead]
+    cols = [spread(x, k + j) for j in range(4)]
     down = [spread(y, k + j) for j in range(4)]
-    for j, tile in enumerate([*cols, *coming, x]):
+    for j, tile in enumerate([*cols, x]):
         hold[j * SUB:(j + 1) * SUB] = tile
     line = lambda j, i: hold[pl.ds(j * SUB + at + i, SUB, stride=0)]
     a0, a1, a2 = line(0, 0), line(1, 0), line(1, 1)
@@ -73,29 +71,18 @@
     s2 = det * c2 - (g10 * b10 + g11 * b11)
     rs = reciprocal(s0 * s2 - s1 * s1)
     ra = reciprocal(det)
-
-    def known(e):
-        t2 = det * e[2] - (g00 * e[0] + g01 * e[1])
-        t3 = det * e[3] - (g10 * e[0] + g11 * e[1])
-        return a2 * e[0] - a1 * e[1], a0 * e[1] - a1 * e[0], s2 * t2 - s1 * t3, s0 * t3 - s1 * t2
-
-    def second(c):
-        return c[0], c[1], c[2] - (c[0] * g00 + c[1] * g01) * ra, c[3] - (c[0] * g10 + c[1] * g11) * ra
-
-    def less(base, c, v):
-        return (base - (c[0] * v[0] + c[1] * v[1]) * ra) - (c[2] * v[2] + c[3] * v[3]) * rs
-
-    cols = second([jnp.where(own, jnp.where(row == at + j, -1.0, 0.0), cols[j]) for j in range(4)])
-    down = second(down)
-    there = [known([line(4 + j, i) for i in range(4)]) for j in range(4)]
-    if at + 4 < SUB:
-        after = [less(jnp.where(own, 0.0, coming[j]), cols, there[j]) for j in range(4)]
-    else:
-        after = [less(spread(y, ahead[j]), down, there[j]) for j in range(4)]
-    here = known([jnp.where(inside, jnp.where(lane == k + j, 1.0, 0.0), line(8, j)) for j in range(4)])
-    x = less(jnp.where(inside | own, 0.0, x), cols, here)
-    y = less(jnp.where(inside, 0.0, y), down, here)
-    return x, y, after
+    e = [jnp.where(inside, jnp.where(lane == k + j, 1.0, 0.0), line(4, j)) for j in range(4)]
+    t2 = det * e[2] - (g00 * e[0] + g01 * e[1])
+    t3 = det * e[3] - (g10 * e[0] + g11 * e[1])
+    v0, v1 = a2 * e[0] - a1 * e[1], a0 * e[1] - a1 * e[0]
+    v2, v3 = s2 * t2 - s1 * t3, s0 * t3 - s1 * t2
+
+    def less(base, c):
+        c2, c3 = c[2] - (c[0] * g00 + c[1] * g01) * ra, c[3] - (c[0] * g10 + c[1] * g11) * ra
+        return (base - (c[0] * v0 + c[1] * v1) * ra) - (c2 * v2 + c3 * v3) * rs
+
+    cols = [jnp.where(own, jnp.where(row == at + j, -1.0, 0.0), cols[j]) for j in range(4)]
+    return less(jnp.where(inside | own, 0.0, x), cols), less(jnp.where(inside, 0.0, y), down)
 
 
 def invert(m, xt, w6, hold):
@@ -106,41 +93,35 @@
     eye = jnp.where(wide == lax.broadcasted_iota(jnp.int32, (size, size), 0), 1.0, 0.0).astype(BF16)
     count = size // SUB
 
-    def trail(t):
-        k = t * SUB
-        u = jnp.dot(xt[...], w6[...], preferred_element_type=F32)
-        new = jnp.where((wide >= k) & (wide < k + SUB), 0.0, m[...]) - u
+    def trail():
+        new = m[...] - jnp.dot(xt[...], w6[...], preferred_element_type=F32)
         m[...] = new
         return new
 
-    def step(t, carry):
-        x, *cols = carry
+    x, y = m[0:SUB], m[SUB:2 * SUB]
+    for t in range(count):
         k = t * SUB
-        after = (t + 1) % count * SUB
-        y = trail(t - 1)[after:after + SUB] if t else m[SUB:2 * SUB]
-        z = jnp.where(lane < k, -1.0, 1.0) * x
-        z = jnp.where((lane >= k) & (lane < k + SUB), jnp.where(lane - k == row, -1.0, 0.0), z)
+        if t:
+            after = (t + 1) % count * SUB
+            y = trail()[after:after + SUB]
+        unit = jnp.where(lane - row == k, 1.0, 0.0)
+        z = jnp.where((lane >= k) & (lane < k + SUB), -unit, jnp.where(lane < k, -x, x))
         h, n, l = parts(z)
         z = jnp.concatenate([h, h, n, n, h, l], axis=0).astype(BF16)
         xt[...] = lax.dot_general(eye, z, (((1,), (1,)), ((), ())), preferred_element_type=F32).astype(BF16)
         for g in range(0, SUB, 4):
-            x, y, cols = four(x, y, cols, g, k + g, lane, row, hold.at[g // 4])
-        h, n, l = parts(x)
+            x, y = four(x, y, g, k + g, lane, row, hold.at[g // 4])
+        h, n, l = parts(x + unit)
         w6[...] = jnp.concatenate([h, n, h, n, l, h], axis=0).astype(BF16)
-        m[pl.ds(k, SUB)] = jnp.zeros((SUB, size), F32)
-        return y, *cols
-
-    x = m[0:SUB]
-    carry = (x, *(spread(x, j) for j in range(4)))
-    for t in range(count):
-        carry = step(t, carry)
-    trail(count - 1)
+        m[k:k + SUB] = -unit
+        x = y
+    trail()
 
 
 def invert_scratch(size):
     return [
         pltpu.VMEM((size, size), F32), pltpu.VMEM((size, 6 * SUB), BF16), pltpu.VMEM((6 * SUB, size), BF16),
-        pltpu.VMEM((SUB // 4, 10 * SUB, size), F32),
+        pltpu.VMEM((SUB // 4, 6 * SUB, size), F32),
     ]
 
 

time: 31.1 us -> 33.5 us (1.077)
  the two profiles are of different devices: /device:TPU:0 before, /device:TPU:24 now
where the time goes in v1:
time: 33.5 us; the launch traced here: 33.4 us
  Pallas kernels  21.7 us (65%)
  starting transfers between devices  7.33 us (22%)
  waiting for transfers between devices  4.25 us (13%)
    pallas_call x8, Pallas kernels, call(): pl.pallas_call(kernel, out_shape=[jax.ShapeDtypeStruct(getattr(out, 'shap...  21.7 us
    ppermute x6, starting transfers between devices, from_partner(): lax.ppermute(block, axis, [(i, i ^ 1 << apart) for i in range(count)])  7.33 us
    ppermute x6, waiting for transfers between devices, from_partner(): lax.ppermute(block, axis, [(i, i ^ 1 << apart) for i in range(count)])  4.25 us
  transfers between devices with their start and end apart: 6, of which 2 were waited for; matrix products, arithmetic and copies ran while one was open for 0% of the time, Pallas kernels for 55%

profile of v1, /device:TPU:24, one launch (start us, length us, event | category | flops | bytes accessed | tf_op | source)
XLA Modules:
  0.0 33.4 jit_solution(7157477069260514591)
XLA Ops:
  0.0 0.0 copy-start
  0.0 2.1 %shard_map.64 = (bf16[512,512]{1,0:T(8,128)(2,1)S(1)}, bf16[512,512]{1,0:T(8,128)(2,1)S(1)}, f32[128,512]{1,0:T(8,128)S(1)}, s32[1,512]{1,0:T(1,128)S(1)}, f32[5...) custom-call(f32[512,512]{1,0:T(8,128)} %inverse_far.1, f32[512,128]{1,0:T(8,128)} %basis_far.1, s32[1,512]{1,0:T(1,128)} %order_far.1), custom_call_target="tpu_custom_call" | custom-call | flops 1000000000 | tf_op jit(solution)/shard_map/pallas_call | solution.py:265
  2.1 1.6 %collective-permute-start.1 = (f32[72,128]{1,0:T(8,128)S(1)}, f32[72,128]{1,0:T(8,128)S(1)}, u32[]{:S(2)}, u32[]{:S(2)}) collective-permute-start(f32[72,128]{1,0:T(8,128)S(1)} %get-tuple-element.32.gram), channel_id=1, source_target_pairs={{0,4},{4,0},{8,12},{12,8},{16,20},{20,16},{24,28},{28,24},{1,5},{5... | collective-permute-start | bytes 110600 | tf_op jit(solution)/shard_map/ppermute | solution.py:278
  3.7 0.0 copy-done
  3.7 1.8 %shard_map.65 = (f32[512,256]{1,0:T(8,128)S(1)}, f32[128,256]{1,0:T(8,128)S(1)}) custom-call(s32[1,512]{1,0:T(1,128)S(1)} %get-tuple-element.27.order.refs_4_, f32[512,256]{1,0:T(8,128)S(1)} %copy-done, bf16[512,512]{1,0:T(8,128)(2,1)S(1)} %get-tuple-element.28.top, bf16[512,512]{1,0:T(8,128)(2,1)S(1)} %get-tuple-element.29.low, ...), custom_call_target="tpu_custom_call" | custom-call | flops 2000000000 | tf_op jit(solution)/shard_map/pallas_call | solution.py:265
  5.5 0.6 %collective-permute-start = (f32[128,256]{1,0:T(8,128)S(1)}, f32[128,256]{1,0:T(8,128)S(1)}, u32[]{:S(2)}, u32[]{:S(2)}) collective-permute-start(f32[128,256]{1,0:T(8,128)S(1)} %get-tuple-element.31.refs_0_), channel_id=1, source_target_pairs={{0,4},{4,0},{8,12},{12,8},{16,20},{20,16},{24,28},{28,24},{1,5},{5... | collective-permute-start | bytes 393224 | tf_op jit(solution)/shard_map/ppermute | solution.py:278
  6.0 0.0 collective-permute-done.1.other
  6.1 0.0 copy-done.1
  6.1 0.0 copy-done.2
  6.1 5.1 %shard_map.66 = (f32[128,128]{1,0:T(8,128)S(1)}, f32[128,128]{1,0:T(8,128)S(1)}, f32[72,128]{1,0:T(8,128)S(1)}) custom-call(f32[72,128]{1,0:T(8,128)S(1)} %get-tuple-element.32.gram, f32[72,128]{1,0:T(8,128)S(1)} %collective-permute-done.1.other, bf16[1,3,128,128]{3,2,1,0:T(8,128)(2,1)S(1)} %copy-done.1, bf16[1,2,128,128]{3,2,1,0:T(8,128)(2,1)S(1)} %copy-done.2), custom_call_target="tpu_custom_call" | custom-call | flops 6000000000 | tf_op jit(solution)/shard_map/pallas_call | solution.py:265
  11.2 0.5 %collective-permute-start.3 = (f32[72,128]{1,0:T(8,128)S(1)}, f32[72,128]{1,0:T(8,128)S(1)}, u32[]{:S(2)}, u32[]{:S(2)}) collective-permute-start(f32[72,128]{1,0:T(8,128)S(1)} %get-tuple-element.38.gram), channel_id=1, source_target_pairs={{0,8},{4,12},{8,0},{12,4},{16,24},{20,28},{24,16},{28,20},{1,9},{5... | collective-permute-start | bytes 110600 | tf_op jit(solution)/shard_map/ppermute | solution.py:278
  11.7 0.0 collective-permute-done.refs_1_
  11.7 0.8 %shard_map.67 = (f32[128,256]{1,0:T(8,128)S(1)}, f32[128,256]{1,0:T(8,128)S(1)}, f32[128,128]{1,0:T(8,128)S(1)}, f32[512,256]{1,0:T(8,128)S(1)}, f32[512,128]{1,0:T(8,128)S(1)}) custom-call(f32[128,256]{1,0:T(8,128)S(1)} %get-tuple-element.31.refs_0_, f32[128,256]{1,0:T(8,128)S(1)} %collective-permute-done.refs_1_, ...), custom_call_target="tpu_custom_call" | custom-call | flops 1000000000 | tf_op jit(solution)/shard_map/pallas_call | solution.py:265
  12.5 1.6 %collective-permute-start.2 = (f32[128,256]{1,0:T(8,128)S(1)}, f32[128,256]{1,0:T(8,128)S(1)}, u32[]{:S(2)}, u32[]{:S(2)}) collective-permute-start(f32[128,256]{1,0:T(8,128)S(1)} %get-tuple-element.37.refs_0_), channel_id=1, source_target_pairs={{0,8},{4,12},{8,0},{12,4},{16,24},{20,28},{24,16},{28,20},{1,9},{5... | collective-permute-start | bytes 393224 | tf_op jit(solution)/shard_map/ppermute | solution.py:278
  14.1 1.4 %collective-permute-done.3.other = f32[72,128]{1,0:T(8,128)S(1)} collective-permute-done((f32[72,128]{1,0:T(8,128)S(1)}, f32[72,128]{1,0:T(8,128)S(1)}, u32[]{:S(2)}, u32[]{:S(2)}) %collective-permute-start.3) | collective-permute-done | bytes 36896 | tf_op jit(solution)/shard_map/ppermute | solution.py:278
  15.5 5.1 %shard_map.68 = (f32[128,128]{1,0:T(8,128)S(1)}, f32[128,128]{1,0:T(8,128)S(1)}, f32[72,128]{1,0:T(8,128)S(1)}) custom-call(f32[72,128]{1,0:T(8,128)S(1)} %get-tuple-element.38.gram, f32[72,128]{1,0:T(8,128)S(1)} %collective-permute-done.3.other, bf16[1,3,128,128]{3,2,1,0:T(8,128)(2,1)S(1)} %copy-done.1, bf16[1,2,128,128]{3,2,1,0:T(8,128)(2,1)S(1)} %copy-done.2), custom_call_target="tpu_custom_call" | custom-call | flops 6000000000 | tf_op jit(solution)/shard_map/pallas_call | solution.py:265
  20.6 0.4 %collective-permute-start.5 = (f32[72,128]{1,0:T(8,128)S(1)}, f32[72,128]{1,0:T(8,128)S(1)}, u32[]{:S(2)}, u32[]{:S(2)}) collective-permute-start(f32[72,128]{1,0:T(8,128)S(1)} %get-tuple-element.46.gram), channel_id=1, source_target_pairs={{0,16},{4,20},{8,24},{12,28},{16,0},{20,4},{24,8},{28,12},{1,17},{... | collective-permute-start | bytes 110600 | tf_op jit(solution)/shard_map/ppermute | solution.py:278
  21.0 0.0 collective-permute-done.2.refs_1_
  21.0 0.9 %shard_map.69 = (f32[128,256]{1,0:T(8,128)S(1)}, f32[512,256]{1,0:T(8,128)S(1)}, f32[512,128]{1,0:T(8,128)S(1)}) custom-call(f32[128,256]{1,0:T(8,128)S(1)} %get-tuple-element.37.refs_0_, f32[128,256]{1,0:T(8,128)S(1)} %collective-permute-done.2.refs_1_, f32[128,128]{1,0:T(8,128)S(1)} %get-tuple-element.39.refs_2_, ...), custom_call_target="tpu_custom_call" | custom-call | flops 1000000000 | tf_op jit(solution)/shard_map/pallas_call | solution.py:265
  21.9 2.6 %collective-permute-start.4 = (f32[128,256]{1,0:T(8,128)S(1)}, f32[128,256]{1,0:T(8,128)S(1)}, u32[]{:S(2)}, u32[]{:S(2)}) collective-permute-start(f32[128,256]{1,0:T(8,128)S(1)} %get-tuple-element.45.projected), channel_id=1, source_target_pairs={{0,16},{4,20},{8,24},{12,28},{16,0},{20,4},{24,8},{28,12},{1,17},{... | collective-permute-start | bytes 393224 | tf_op jit(solution)/shard_map/ppermute | solution.py:278
  24.6 2.8 %collective-permute-done.5.other = f32[72,128]{1,0:T(8,128)S(1)} collective-permute-done((f32[72,128]{1,0:T(8,128)S(1)}, f32[72,128]{1,0:T(8,128)S(1)}, u32[]{:S(2)}, u32[]{:S(2)}) %collective-permute-start.5) | collective-permute-done | bytes 36896 | tf_op jit(solution)/shard_map/ppermute | solution.py:278
  27.4 4.7 %shard_map.70.inverse = f32[128,128]{1,0:T(8,128)S(1)} custom-call(f32[72,128]{1,0:T(8,128)S(1)} %get-tuple-element.46.gram, f32[72,128]{1,0:T(8,128)S(1)} %collective-permute-done.5.other, bf16[1,3,128,128]{3,2,1,0:T(8,128)(2,1)S(1)} %copy-done.1), custom_call_target="tpu_custom_call" | custom-call | flops 6000000000 | tf_op jit(solution)/shard_map/pallas_call | solution.py:265
  32.1 0.0 collective-permute-done.4.other
  32.1 1.3 %shard_map.71 = f32[512,256]{1,0:T(8,128)} custom-call(f32[128,256]{1,0:T(8,128)S(1)} %get-tuple-element.45.projected, f32[128,256]{1,0:T(8,128)S(1)} %collective-permute-done.4.other, f32[128,128]{1,0:T(8,128)S(1)} %shard_map.70.inverse, f32[512,256]{1,0:T(8,128)S(1)} %get-tuple-element.47.solved, f32[512,128]{1,0:T(8,128)S(1)} %get-tuple-element.48.carried), custom_call_target="tpu_custom_call" | custom-call | flops 1000000000 | tf_op jit(solution)/shard_map/pallas_call | solution.py:265
  (2 shorter events, 0.0 us)
Async XLA Ops:
  0.0 3.7 %copy-start = (f32[512,256]{1,0:T(8,128)S(1)}, f32[512,256]{1,0:T(8,128)}, u32[]{:S(2)}) copy-start(f32[512,256]{1,0:T(8,128)} %rhs.1) | copy-start | bytes 1572868
  2.1 4.0 %collective-permute-start.1 = (f32[72,128]{1,0:T(8,128)S(1)}, f32[72,128]{1,0:T(8,128)S(1)}, u32[]{:S(2)}, u32[]{:S(2)}) collective-permute-start(f32[72,128]{1,0:T(8,128)S(1)} %get-tuple-element.32.gram), channel_id=1, source_target_pairs={{0,4},{4,0},{8,12},{12,8},{16,20},{20,16},{24,28},{28,24},{1,5},{5... | collective-permute-start | bytes 110600 | tf_op jit(solution)/shard_map/ppermute | solution.py:278
  3.7 2.4 %copy-start.1 = (bf16[1,3,128,128]{3,2,1,0:T(8,128)(2,1)S(1)}, bf16[1,3,128,128]{3,2,1,0:T(8,128)(2,1)}, u32[]{:S(2)}) copy-start(bf16[1,3,128,128]{3,2,1,0:T(8,128)(2,1)} %precision.5) | copy-start | bytes 294916
  3.7 2.4 %copy-start.2 = (bf16[1,2,128,128]{3,2,1,0:T(8,128)(2,1)S(1)}, bf16[1,2,128,128]{3,2,1,0:T(8,128)(2,1)}, u32[]{:S(2)}) copy-start(bf16[1,2,128,128]{3,2,1,0:T(8,128)(2,1)} %rest_0_.3) | copy-start | bytes 196612
  5.5 6.2 %collective-permute-start = (f32[128,256]{1,0:T(8,128)S(1)}, f32[128,256]{1,0:T(8,128)S(1)}, u32[]{:S(2)}, u32[]{:S(2)}) collective-permute-start(f32[128,256]{1,0:T(8,128)S(1)} %get-tuple-element.31.refs_0_), channel_id=1, source_target_pairs={{0,4},{4,0},{8,12},{12,8},{16,20},{20,16},{24,28},{28,24},{1,5},{5... | collective-permute-start | bytes 393224 | tf_op jit(solution)/shard_map/ppermute | solution.py:278
  11.2 4.3 %collective-permute-start.3 = (f32[72,128]{1,0:T(8,128)S(1)}, f32[72,128]{1,0:T(8,128)S(1)}, u32[]{:S(2)}, u32[]{:S(2)}) collective-permute-start(f32[72,128]{1,0:T(8,128)S(1)} %get-tuple-element.38.gram), channel_id=1, source_target_pairs={{0,8},{4,12},{8,0},{12,4},{16,24},{20,28},{24,16},{28,20},{1,9},{5... | collective-permute-start | bytes 110600 | tf_op jit(solution)/shard_map/ppermute | solution.py:278
  12.5 8.5 %collective-permute-start.2 = (f32[128,256]{1,0:T(8,128)S(1)}, f32[128,256]{1,0:T(8,128)S(1)}, u32[]{:S(2)}, u32[]{:S(2)}) collective-permute-start(f32[128,256]{1,0:T(8,128)S(1)} %get-tuple-element.37.refs_0_), channel_id=1, source_target_pairs={{0,8},{4,12},{8,0},{12,4},{16,24},{20,28},{24,16},{28,20},{1,9},{5... | collective-permute-start | bytes 393224 | tf_op jit(solution)/shard_map/ppermute | solution.py:278
  20.6 6.8 %collective-permute-start.5 = (f32[72,128]{1,0:T(8,128)S(1)}, f32[72,128]{1,0:T(8,128)S(1)}, u32[]{:S(2)}, u32[]{:S(2)}) collective-permute-start(f32[72,128]{1,0:T(8,128)S(1)} %get-tuple-element.46.gram), channel_id=1, source_target_pairs={{0,16},{4,20},{8,24},{12,28},{16,0},{20,4},{24,8},{28,12},{1,17},{... | collective-permute-start | bytes 110600 | tf_op jit(solution)/shard_map/ppermute | solution.py:278
  21.9 10.1 %collective-permute-start.4 = (f32[128,256]{1,0:T(8,128)S(1)}, f32[128,256]{1,0:T(8,128)S(1)}, u32[]{:S(2)}, u32[]{:S(2)}) collective-permute-start(f32[128,256]{1,0:T(8,128)S(1)} %get-tuple-element.45.projected), channel_id=1, source_target_pairs={{0,16},{4,20},{8,24},{12,28},{16,0},{20,4},{24,8},{28,12},{1,17},{... | collective-permute-start | bytes 393224 | tf_op jit(solution)/shard_map/ppermute | solution.py:278

commit v2 on v1

--- a/solution.py
+++ b/solution.py
@@ -51,13 +51,14 @@
     return jnp.broadcast_to(x[:, k:k + 1], x.shape)
 
 
-def four(x, y, at, k, lane, row, hold):
+def four(x, y, cols, at, k, lane, row, hold):
     size = x.shape[1]
     inside = (lane >= k) & (lane < k + 4)
     own = (row >= at) & (row < at + 4)
-    cols = [spread(x, k + j) for j in range(4)]
+    ahead = [(k + 4 + j) % size for j in range(4)]
+    coming = [spread(x, a) for a in ahead]
     down = [spread(y, k + j) for j in range(4)]
-    for j, tile in enumerate([*cols, x]):
+    for j, tile in enumerate([*cols, *coming, x]):
         hold[j * SUB:(j + 1) * SUB] = tile
     line = lambda j, i: hold[pl.ds(j * SUB + at + i, SUB, stride=0)]
     a0, a1, a2 = line(0, 0), line(1, 0), line(1, 1)
@@ -71,18 +72,27 @@
     s2 = det * c2 - (g10 * b10 + g11 * b11)
     rs = reciprocal(s0 * s2 - s1 * s1)
     ra = reciprocal(det)
-    e = [jnp.where(inside, jnp.where(lane == k + j, 1.0, 0.0), line(4, j)) for j in range(4)]
-    t2 = det * e[2] - (g00 * e[0] + g01 * e[1])
-    t3 = det * e[3] - (g10 * e[0] + g11 * e[1])
-    v0, v1 = a2 * e[0] - a1 * e[1], a0 * e[1] - a1 * e[0]
-    v2, v3 = s2 * t2 - s1 * t3, s0 * t3 - s1 * t2
-
-    def less(base, c):
-        c2, c3 = c[2] - (c[0] * g00 + c[1] * g01) * ra, c[3] - (c[0] * g10 + c[1] * g11) * ra
-        return (base - (c[0] * v0 + c[1] * v1) * ra) - (c2 * v2 + c3 * v3) * rs
-
-    cols = [jnp.where(own, jnp.where(row == at + j, -1.0, 0.0), cols[j]) for j in range(4)]
-    return less(jnp.where(inside | own, 0.0, x), cols), less(jnp.where(inside, 0.0, y), down)
+
+    def left(c):
+        f0, f1 = (a2 * c[0] - a1 * c[1]) * ra, (a0 * c[1] - a1 * c[0]) * ra
+        p2, p3 = c[2] - (f0 * b00 + f1 * b01), c[3] - (f0 * b10 + f1 * b11)
+        return f0, f1, s2 * p2 - s1 * p3, s0 * p3 - s1 * p2
+
+    def right(e):
+        return e[0], e[1], det * e[2] - (g00 * e[0] + g01 * e[1]), det * e[3] - (g10 * e[0] + g11 * e[1])
+
+    def less(base, c, e):
+        return (base - (c[0] * e[0] + c[1] * e[1])) - (c[2] * e[2] + c[3] * e[3]) * rs
+
+    cols = left([jnp.where(own, jnp.where(row == at + j, -1.0, 0.0), cols[j]) for j in range(4)])
+    down = left(down)
+    there = [right([line(4 + j, i) for i in range(4)]) for j in range(4)]
+    if at + 4 < SUB:
+        after = [less(jnp.where(own, 0.0, coming[j]), cols, there[j]) for j in range(4)]
+    else:
+        after = [less(spread(y, ahead[j]), down, there[j]) for j in range(4)]
+    here = right([jnp.where(inside, jnp.where(lane == k + j, 1.0, 0.0), line(8, j)) for j in range(4)])
+    return less(jnp.where(inside | own, 0.0, x), cols, here), less(jnp.where(inside, 0.0, y), down, here), after
 
 
 def invert(m, xt, w6, hold):
@@ -99,18 +109,20 @@
         return new
 
     x, y = m[0:SUB], m[SUB:2 * SUB]
+    cols = [spread(x, j) for j in range(4)]
     for t in range(count):
         k = t * SUB
         if t:
             after = (t + 1) % count * SUB
             y = trail()[after:after + SUB]
         unit = jnp.where(lane - row == k, 1.0, 0.0)
-        z = jnp.where((lane >= k) & (lane < k + SUB), -unit, jnp.where(lane < k, -x, x))
+        panel = (lane >= k) & (lane < k + SUB)
+        z = jnp.where(panel, -unit, jnp.where(lane < k, -x, x))
         h, n, l = parts(z)
         z = jnp.concatenate([h, h, n, n, h, l], axis=0).astype(BF16)
         xt[...] = lax.dot_general(eye, z, (((1,), (1,)), ((), ())), preferred_element_type=F32).astype(BF16)
         for g in range(0, SUB, 4):
-            x, y = four(x, y, g, k + g, lane, row, hold.at[g // 4])
+            x, y, cols = four(x, y, cols, g, k + g, lane, row, hold.at[g // 4])
         h, n, l = parts(x + unit)
         w6[...] = jnp.concatenate([h, n, h, n, l, h], axis=0).astype(BF16)
         m[k:k + SUB] = -unit
@@ -121,7 +133,7 @@
 def invert_scratch(size):
     return [
         pltpu.VMEM((size, size), F32), pltpu.VMEM((size, 6 * SUB), BF16), pltpu.VMEM((6 * SUB, size), BF16),
-        pltpu.VMEM((SUB // 4, 6 * SUB, size), F32),
+        pltpu.VMEM((SUB // 4, 10 * SUB, size), F32),
     ]
 
 

time: 33.5 us -> 31.1 us (0.928)
  the two profiles are of different devices: /device:TPU:24 before, /device:TPU:0 now
where the time goes in v2:
time: 31.1 us; the launch traced here: 30.9 us
  Pallas kernels  19.2 us (62%)
  starting transfers between devices  8.62 us (28%)
  waiting for transfers between devices  3.04 us (10%)
    pallas_call x8, Pallas kernels, call(): pl.pallas_call(kernel, out_shape=[jax.ShapeDtypeStruct(getattr(out, 'shap...  19.2 us
    ppermute x6, starting transfers between devices, from_partner(): lax.ppermute(block, axis, [(i, i ^ 1 << apart) for i in range(count)])  8.62 us
    ppermute x6, waiting for transfers between devices, from_partner(): lax.ppermute(block, axis, [(i, i ^ 1 << apart) for i in range(count)])  3.04 us
  transfers between devices with their start and end apart: 6, of which 3 were waited for; matrix products, arithmetic and copies ran while one was open for 0% of the time, Pallas kernels for 51%

profile of v2, /device:TPU:0, one launch (start us, length us, event | category | flops | bytes accessed | tf_op | source)
XLA Modules:
  0.0 30.9 jit_solution(5971933636677219170)
XLA Ops:
  0.0 0.0 copy-start
  0.0 2.1 %shard_map.64 = (bf16[512,512]{1,0:T(8,128)(2,1)S(1)}, bf16[512,512]{1,0:T(8,128)(2,1)S(1)}, f32[128,512]{1,0:T(8,128)S(1)}, s32[1,512]{1,0:T(1,128)S(1)}, f32[5...) custom-call(f32[512,512]{1,0:T(8,128)} %inverse_far.1, f32[512,128]{1,0:T(8,128)} %basis_far.1, s32[1,512]{1,0:T(1,128)} %order_far.1), custom_call_target="tpu_custom_call" | custom-call | flops 1000000000 | tf_op jit(solution)/shard_map/pallas_call | solution.py:277
  2.1 3.0 %collective-permute-start.1 = (f32[72,128]{1,0:T(8,128)S(1)}, f32[72,128]{1,0:T(8,128)S(1)}, u32[]{:S(2)}, u32[]{:S(2)}) collective-permute-start(f32[72,128]{1,0:T(8,128)S(1)} %get-tuple-element.32.gram), channel_id=1, source_target_pairs={{0,4},{4,0},{8,12},{12,8},{16,20},{20,16},{24,28},{28,24},{1,5},{5... | collective-permute-start | bytes 110600 | tf_op jit(solution)/shard_map/ppermute | solution.py:290
  5.1 0.0 copy-done
  5.1 1.8 %shard_map.65 = (f32[512,256]{1,0:T(8,128)S(1)}, f32[128,256]{1,0:T(8,128)S(1)}) custom-call(s32[1,512]{1,0:T(1,128)S(1)} %get-tuple-element.27.order.refs_4_, f32[512,256]{1,0:T(8,128)S(1)} %copy-done, bf16[512,512]{1,0:T(8,128)(2,1)S(1)} %get-tuple-element.28.top, bf16[512,512]{1,0:T(8,128)(2,1)S(1)} %get-tuple-element.29.low, ...), custom_call_target="tpu_custom_call" | custom-call | flops 2000000000 | tf_op jit(solution)/shard_map/pallas_call | solution.py:277
  6.9 0.1 collective-permute-start
  7.0 0.0 collective-permute-done.1.other
  7.0 0.0 copy-done.1
  7.0 0.0 copy-done.2
  7.0 4.2 %shard_map.66 = (f32[128,128]{1,0:T(8,128)S(1)}, f32[128,128]{1,0:T(8,128)S(1)}, f32[72,128]{1,0:T(8,128)S(1)}) custom-call(f32[72,128]{1,0:T(8,128)S(1)} %get-tuple-element.32.gram, f32[72,128]{1,0:T(8,128)S(1)} %collective-permute-done.1.other, bf16[1,3,128,128]{3,2,1,0:T(8,128)(2,1)S(1)} %copy-done.1, bf16[1,2,128,128]{3,2,1,0:T(8,128)(2,1)S(1)} %copy-done.2), custom_call_target="tpu_custom_call" | custom-call | flops 6000000000 | tf_op jit(solution)/shard_map/pallas_call | solution.py:277
  11.3 2.1 %collective-permute-start.3 = (f32[72,128]{1,0:T(8,128)S(1)}, f32[72,128]{1,0:T(8,128)S(1)}, u32[]{:S(2)}, u32[]{:S(2)}) collective-permute-start(f32[72,128]{1,0:T(8,128)S(1)} %get-tuple-element.38.gram), channel_id=1, source_target_pairs={{0,8},{4,12},{8,0},{12,4},{16,24},{20,28},{24,16},{28,20},{1,9},{5... | collective-permute-start | bytes 110600 | tf_op jit(solution)/shard_map/ppermute | solution.py:290
  13.4 0.0 collective-permute-done.refs_1_
  13.4 0.8 %shard_map.67 = (f32[128,256]{1,0:T(8,128)S(1)}, f32[128,256]{1,0:T(8,128)S(1)}, f32[128,128]{1,0:T(8,128)S(1)}, f32[512,256]{1,0:T(8,128)S(1)}, f32[512,128]{1,0:T(8,128)S(1)}) custom-call(f32[128,256]{1,0:T(8,128)S(1)} %get-tuple-element.31.refs_0_, f32[128,256]{1,0:T(8,128)S(1)} %collective-permute-done.refs_1_, ...), custom_call_target="tpu_custom_call" | custom-call | flops 1000000000 | tf_op jit(solution)/shard_map/pallas_call | solution.py:277
  14.3 0.2 collective-permute-start.2
  14.4 1.0 %collective-permute-done.3.other = f32[72,128]{1,0:T(8,128)S(1)} collective-permute-done((f32[72,128]{1,0:T(8,128)S(1)}, f32[72,128]{1,0:T(8,128)S(1)}, u32[]{:S(2)}, u32[]{:S(2)}) %collective-permute-start.3) | collective-permute-done | bytes 36896 | tf_op jit(solution)/shard_map/ppermute | solution.py:290
  15.4 4.2 %shard_map.68 = (f32[128,128]{1,0:T(8,128)S(1)}, f32[128,128]{1,0:T(8,128)S(1)}, f32[72,128]{1,0:T(8,128)S(1)}) custom-call(f32[72,128]{1,0:T(8,128)S(1)} %get-tuple-element.38.gram, f32[72,128]{1,0:T(8,128)S(1)} %collective-permute-done.3.other, bf16[1,3,128,128]{3,2,1,0:T(8,128)(2,1)S(1)} %copy-done.1, bf16[1,2,128,128]{3,2,1,0:T(8,128)(2,1)S(1)} %copy-done.2), custom_call_target="tpu_custom_call" | custom-call | flops 6000000000 | tf_op jit(solution)/shard_map/pallas_call | solution.py:277
  19.6 3.1 %collective-permute-start.5 = (f32[72,128]{1,0:T(8,128)S(1)}, f32[72,128]{1,0:T(8,128)S(1)}, u32[]{:S(2)}, u32[]{:S(2)}) collective-permute-start(f32[72,128]{1,0:T(8,128)S(1)} %get-tuple-element.46.gram), channel_id=1, source_target_pairs={{0,16},{4,20},{8,24},{12,28},{16,0},{20,4},{24,8},{28,12},{1,17},{... | collective-permute-start | bytes 110600 | tf_op jit(solution)/shard_map/ppermute | solution.py:290
  22.7 0.0 collective-permute-done.2.refs_1_
  22.7 0.9 %shard_map.69 = (f32[128,256]{1,0:T(8,128)S(1)}, f32[512,256]{1,0:T(8,128)S(1)}, f32[512,128]{1,0:T(8,128)S(1)}) custom-call(f32[128,256]{1,0:T(8,128)S(1)} %get-tuple-element.37.refs_0_, f32[128,256]{1,0:T(8,128)S(1)} %collective-permute-done.2.refs_1_, f32[128,128]{1,0:T(8,128)S(1)} %get-tuple-element.39.refs_2_, ...), custom_call_target="tpu_custom_call" | custom-call | flops 1000000000 | tf_op jit(solution)/shard_map/pallas_call | solution.py:277
  23.7 0.1 collective-permute-start.4
  23.7 0.9 %collective-permute-done.5.other = f32[72,128]{1,0:T(8,128)S(1)} collective-permute-done((f32[72,128]{1,0:T(8,128)S(1)}, f32[72,128]{1,0:T(8,128)S(1)}, u32[]{:S(2)}, u32[]{:S(2)}) %collective-permute-start.5) | collective-permute-done | bytes 36896 | tf_op jit(solution)/shard_map/ppermute | solution.py:290
  24.7 3.8 %shard_map.70.inverse = f32[128,128]{1,0:T(8,128)S(1)} custom-call(f32[72,128]{1,0:T(8,128)S(1)} %get-tuple-element.46.gram, f32[72,128]{1,0:T(8,128)S(1)} %collective-permute-done.5.other, bf16[1,3,128,128]{3,2,1,0:T(8,128)(2,1)S(1)} %copy-done.1), custom_call_target="tpu_custom_call" | custom-call | flops 6000000000 | tf_op jit(solution)/shard_map/pallas_call | solution.py:277
  28.5 1.1 %collective-permute-done.4.other = f32[128,256]{1,0:T(8,128)S(1)} collective-permute-done((f32[128,256]{1,0:T(8,128)S(1)}, f32[128,256]{1,0:T(8,128)S(1)}, u32[]{:S(2)}, u32[]{:S(2)}) %collective-permute-start.4) | collective-permute-done | bytes 131104 | tf_op jit(solution)/shard_map/ppermute | solution.py:290
  29.6 1.3 %shard_map.71 = f32[512,256]{1,0:T(8,128)} custom-call(f32[128,256]{1,0:T(8,128)S(1)} %get-tuple-element.45.projected, f32[128,256]{1,0:T(8,128)S(1)} %collective-permute-done.4.other, f32[128,128]{1,0:T(8,128)S(1)} %shard_map.70.inverse, f32[512,256]{1,0:T(8,128)S(1)} %get-tuple-element.47.solved, f32[512,128]{1,0:T(8,128)S(1)} %get-tuple-element.48.carried), custom_call_target="tpu_custom_call" | custom-call | flops 1000000000 | tf_op jit(solution)/shard_map/pallas_call | solution.py:277
  (2 shorter events, 0.0 us)
Async XLA Ops:
  0.0 5.1 %copy-start = (f32[512,256]{1,0:T(8,128)S(1)}, f32[512,256]{1,0:T(8,128)}, u32[]{:S(2)}) copy-start(f32[512,256]{1,0:T(8,128)} %rhs.1) | copy-start | bytes 1572868
  2.1 5.0 %collective-permute-start.1 = (f32[72,128]{1,0:T(8,128)S(1)}, f32[72,128]{1,0:T(8,128)S(1)}, u32[]{:S(2)}, u32[]{:S(2)}) collective-permute-start(f32[72,128]{1,0:T(8,128)S(1)} %get-tuple-element.32.gram), channel_id=1, source_target_pairs={{0,4},{4,0},{8,12},{12,8},{16,20},{20,16},{24,28},{28,24},{1,5},{5... | collective-permute-start | bytes 110600 | tf_op jit(solution)/shard_map/ppermute | solution.py:290
  5.1 1.9 %copy-start.1 = (bf16[1,3,128,128]{3,2,1,0:T(8,128)(2,1)S(1)}, bf16[1,3,128,128]{3,2,1,0:T(8,128)(2,1)}, u32[]{:S(2)}) copy-start(bf16[1,3,128,128]{3,2,1,0:T(8,128)(2,1)} %precision.5) | copy-start | bytes 294916
  5.1 1.9 %copy-start.2 = (bf16[1,2,128,128]{3,2,1,0:T(8,128)(2,1)S(1)}, bf16[1,2,128,128]{3,2,1,0:T(8,128)(2,1)}, u32[]{:S(2)}) copy-start(bf16[1,2,128,128]{3,2,1,0:T(8,128)(2,1)} %rest_0_.3) | copy-start | bytes 196612
  6.9 6.5 %collective-permute-start = (f32[128,256]{1,0:T(8,128)S(1)}, f32[128,256]{1,0:T(8,128)S(1)}, u32[]{:S(2)}, u32[]{:S(2)}) collective-permute-start(f32[128,256]{1,0:T(8,128)S(1)} %get-tuple-element.31.refs_0_), channel_id=1, source_target_pairs={{0,4},{4,0},{8,12},{12,8},{16,20},{20,16},{24,28},{28,24},{1,5},{5... | collective-permute-start | bytes 393224 | tf_op jit(solution)/shard_map/ppermute | solution.py:290
  11.3 4.1 %collective-permute-start.3 = (f32[72,128]{1,0:T(8,128)S(1)}, f32[72,128]{1,0:T(8,128)S(1)}, u32[]{:S(2)}, u32[]{:S(2)}) collective-permute-start(f32[72,128]{1,0:T(8,128)S(1)} %get-tuple-element.38.gram), channel_id=1, source_target_pairs={{0,8},{4,12},{8,0},{12,4},{16,24},{20,28},{24,16},{28,20},{1,9},{5... | collective-permute-start | bytes 110600 | tf_op jit(solution)/shard_map/ppermute | solution.py:290
  14.3 8.5 %collective-permute-start.2 = (f32[128,256]{1,0:T(8,128)S(1)}, f32[128,256]{1,0:T(8,128)S(1)}, u32[]{:S(2)}, u32[]{:S(2)}) collective-permute-start(f32[128,256]{1,0:T(8,128)S(1)} %get-tuple-element.37.refs_0_), channel_id=1, source_target_pairs={{0,8},{4,12},{8,0},{12,4},{16,24},{20,28},{24,16},{28,20},{1,9},{5... | collective-permute-start | bytes 393224 | tf_op jit(solution)/shard_map/ppermute | solution.py:290
  19.6 5.0 %collective-permute-start.5 = (f32[72,128]{1,0:T(8,128)S(1)}, f32[72,128]{1,0:T(8,128)S(1)}, u32[]{:S(2)}, u32[]{:S(2)}) collective-permute-start(f32[72,128]{1,0:T(8,128)S(1)} %get-tuple-element.46.gram), channel_id=1, source_target_pairs={{0,16},{4,20},{8,24},{12,28},{16,0},{20,4},{24,8},{28,12},{1,17},{... | collective-permute-start | bytes 110600 | tf_op jit(solution)/shard_map/ppermute | solution.py:290
  23.7 6.0 %collective-permute-start.4 = (f32[128,256]{1,0:T(8,128)S(1)}, f32[128,256]{1,0:T(8,128)S(1)}, u32[]{:S(2)}, u32[]{:S(2)}) collective-permute-start(f32[128,256]{1,0:T(8,128)S(1)} %get-tuple-element.45.projected), channel_id=1, source_target_pairs={{0,16},{4,20},{8,24},{12,28},{16,0},{20,4},{24,8},{28,12},{1,17},{... | collective-permute-start | bytes 393224 | tf_op jit(solution)/shard_map/ppermute | solution.py:290
